TPU v7x, 32 devices: a whole 2x2x4 slice. The times are simulated.
32 devices in a mesh: pair: 16 (over z, x, core), aux: 2 (over y).
Axes of the slice: x: 2, y: 2, z: 4, core: 2. Of those that a mesh axis runs over, the one named last changes fastest.
Arguments:
- doubles: bfloat16 [32, 512, 512], P('pair', 'aux'), may hold values from -1.796875 to 1.796875
- singles: bfloat16 [256, 512], replicated, may hold values from -0.8984375 to 0.8984375
- vir_slabs: bfloat16 [4096, 8, 512], P(('aux', 'pair')), may hold values from -0.059814453 to 0.059814453
- occ_slabs: bfloat16 [4096, 256, 512], P(('aux', 'pair')), may hold values from -0.029907227 to 0.029907227
- occ_energy: float32 [256], replicated, may hold values from -2 to -0.5
- vir_energy: float32 [8], replicated, may hold values from 0.1 to 1.5
- pair_list: int32 [32, 2], P('pair'), may hold values from 0 to 255
Outputs:
- new_doubles: float32 [32, 8, 8], P('pair', 'aux')
All inputs are finite; a program needn't handle non-finite values.
Results may differ from a plain program's by a relative error of at most 0.0005.
Values may be sent and summed in bfloat16 or wider, within the bound.
A program may use at most 128 MiB of HBM per device.

v0:
```python
import math

import jax
import jax.numpy as jnp
from jax import lax
from jax.sharding import PartitionSpec as P

NWIN = 8


def ladder_block(running, slab_block, tau_amps):
    half_done = jnp.einsum(
        "qac,pcd->pqad", slab_block, tau_amps, preferred_element_type=jnp.float32
    ).astype(jnp.bfloat16)
    return running + jnp.einsum(
        "pqad,qbd->pab", half_done, slab_block, preferred_element_type=jnp.float32
    )


def ladder_rows(running, slab_piece, tau_amps):
    row_count = slab_piece.shape[0]
    block_size = math.gcd(row_count, 64)
    blocks = slab_piece.reshape(
        row_count // block_size, block_size, slab_piece.shape[1], slab_piece.shape[2]
    )

    def one_block(carried, slab_block):
        return (ladder_block(carried, slab_block, tau_amps), None)

    return lax.scan(one_block, running, blocks)[0]


def body(doubles, singles, vir_slabs, occ_slabs, occ_energy, vir_energy, pair_list):
    full_doubles = lax.all_gather(doubles, "aux", axis=1, tiled=True)
    first_occ = pair_list[:, 0]
    second_occ = pair_list[:, 1]
    occ_ids = lax.broadcasted_iota(jnp.int32, (pair_list.shape[0], singles.shape[0]), 1)
    match_first = first_occ[:, None] == occ_ids
    match_second = second_occ[:, None] == occ_ids
    row_first = jnp.dot(
        match_first.astype(jnp.bfloat16), singles, preferred_element_type=jnp.float32
    )
    row_second = jnp.dot(
        match_second.astype(jnp.bfloat16), singles, preferred_element_type=jnp.float32
    )
    tau_amps = (
        full_doubles.astype(jnp.float32) + row_first[:, :, None] * row_second[:, None, :]
    ).astype(jnp.bfloat16)
    dressing_cols = singles[:, :NWIN]
    dressed = (
        vir_slabs.astype(jnp.float32)
        - jnp.einsum("ka,qkc->qac", dressing_cols, occ_slabs, preferred_element_type=jnp.float32)
    ).astype(jnp.bfloat16)
    local_pairs = tau_amps.shape[0]
    empty = jnp.zeros((local_pairs, NWIN, NWIN), jnp.float32)
    gathered = lax.all_gather(dressed, "pair", axis=0, tiled=True)
    partial_value = ladder_rows(empty, gathered, tau_amps)
    share = lax.psum_scatter(partial_value, "aux", scatter_dimension=1, tiled=True)
    share_rows = NWIN // lax.axis_size("aux")
    row_start = lax.axis_index("aux") * share_rows
    own_doubles = lax.dynamic_slice_in_dim(full_doubles[:, :NWIN, :NWIN], row_start, share_rows, 1)
    own_vir = lax.dynamic_slice_in_dim(vir_energy, row_start, share_rows, 0)
    energy_first = jnp.sum(jnp.where(match_first, occ_energy[None, :], 0.0), axis=1)
    energy_second = jnp.sum(jnp.where(match_second, occ_energy[None, :], 0.0), axis=1)
    pair_energy = energy_first + energy_second
    denominator = pair_energy[:, None, None] - own_vir[None, :, None] - vir_energy[None, None, :]
    return own_doubles.astype(jnp.float32) + share / denominator


def solution(mesh):
    placed = (
        P("pair", "aux", None),
        P(),
        P(("aux", "pair"), None, None),
        P(("aux", "pair"), None, None),
        P(),
        P(),
        P("pair", None),
    )
    return jax.shard_map(
        body, mesh=mesh, in_specs=placed, out_specs=P("pair", "aux", None), check_vma=False
    )
```

profile of v0, /device:TPU:0, one launch (start us, length us, event | category | flops | bytes accessed | tf_op | source)
XLA Modules:
  0.0 245.6 jit_solution(1898247297150900595)
XLA Ops:
  7.4 16.6 %fusion.12 = bf16[128,8,512]{2,1,0:T(8,128)(2,1)} fusion(bf16[128,8,512]{2,1,0:T(8,128)(2,1)} %param.11, bf16[128,256,512]{2,1,0:T(8,128)(2,1)} %param.12, bf16[256,512]{1,0:T(8,128)(2,1)} %param.10), kind=kOutput, calls=%fused_computation.10 | convolution fusion | flops 270008320 | bytes 35717120 | tf_op jit(solution)/shard_map/ka,qkc->qac/dot_general | solution.py:52
  26.2 6.7 %all-gather.3.cloned.1.call-done = bf16[2,512,512]{2,1,0:T(8,128)(2,1)} async-done(((bf16[2,256,512]{2,1,0:T(8,128)(2,1)}), bf16[2,512,512]{2,1,0:T(8,128)(2,1)}) %all-gather.3.cloned.1.call-update) | async-done | bytes 1048592 | tf_op jit(solution)/shard_map/all_gather | solution.py:34
  35.2 126.9 %all-gather.5.cloned.1.call-done = bf16[2048,8,512]{2,1,0:T(8,128)(2,1)} async-done(((bf16[128,8,512]{2,1,0:T(8,128)(2,1)}), bf16[2048,8,512]{2,1,0:T(8,128)(2,1)}) %all-gather.5.cloned.1.call-update) | async-done | bytes 16777232 | tf_op jit(solution)/shard_map/all_gather | solution.py:56
  162.0 71.1 %while.11 = (s32[]{:T(128)}, f32[2,8,8]{2,1,0:T(8,128)S(1)}, bf16[32,64,8,512]{3,2,1,0:T(8,128)(2,1)}, bf16[2,512,512]{2,1,0:T(8,128)(2,1)S(1)}, s32[]{:T(128)}, /*index=5*/s32[]{:T(128)}) while((s32[]{:T(128)}, f32[2,8,8]{2,1,0:T(8,128)S(1)}, bf16[32,64,8,512]{3,2,1,0:T(8,128)(2,1)}, bf16[2,512,512]{2,1,0:T(8,128)(2,1)S(1)}, ...), condition=%wide.region_1.2_spmd.clone, body=%wide.region_0.1_spmd.clone.sunk | while | flops 545784064 | bytes 2099798 | solution.py:30
  164.2 2.2 fusion.30
  166.4 2.2 fusion.30
  168.6 2.2 fusion.30
  170.9 2.2 fusion.30
  173.1 2.2 fusion.30
  175.3 2.2 fusion.30
  177.5 2.2 fusion.30
  179.7 2.2 fusion.30
  181.9 2.2 fusion.30
  186.3 2.2 fusion.30
  188.6 2.2 fusion.30
  190.8 2.3 fusion.30
  193.1 2.2 fusion.30
  197.5 2.2 fusion.30
  199.7 2.2 fusion.30
  202.0 2.2 fusion.30
  204.2 2.2 fusion.30
  206.4 2.2 fusion.30
  213.0 2.2 fusion.30
  215.2 2.2 fusion.30
  217.4 2.2 fusion.30
  219.7 2.2 fusion.30
  221.9 2.2 fusion.30
  224.1 2.2 fusion.30
  226.3 2.2 fusion.30
  228.6 2.3 fusion.30
  230.9 2.2 fusion.30
  233.1 5.0 %all-reduce = f32[2,8,8]{2,1,0:T(8,128)S(1)} all-reduce(f32[2,8,8]{2,1,0:T(8,128)S(1)} %get-tuple-element.27), channel_id=2, replica_groups=mesh['pair'=16,'aux'=2] {'aux'}, use_global_device_ids=true, to_apply=%region_2.3.clone | all-reduce | flops 128 | bytes 1024
  (31 shorter events, 16.1 us)
Async XLA Ops:
  6.5 26.4 %all-gather.3.cloned.1.call-start = ((), (), s32[]{:S(2)}) async-start(), calls=%async_computation | async-start | bytes 1572864 | tf_op jit(solution)/shard_map/all_gather | solution.py:34
  7.3 16.8 %copy-start.4 = (u32[32]{0:T(128)S(1)}, u32[32]{0:T(128)}, u32[]{:S(2)}) copy-start(u32[32]{0:T(128)} %constant.24) | copy-start | bytes 388
  7.3 18.0 %copy-start.3 = (f32[8]{0:T(128)S(1)}, f32[8]{0:T(128)}, u32[]{:S(2)}) copy-start(f32[8]{0:T(128)} %param.14) | copy-start | bytes 100
  7.3 18.1 %copy-start.1 = (s32[2,2]{1,0:T(2,128)S(1)}, s32[2,2]{1,0:T(2,128)}, u32[]{:S(2)}) copy-start(s32[2,2]{1,0:T(2,128)} %param.15) | copy-start | bytes 52
  7.3 18.2 %copy-start.2 = (f32[256]{0:T(256)S(1)}, f32[256]{0:T(256)}, u32[]{:S(2)}) copy-start(f32[256]{0:T(256)} %param.13) | copy-start | bytes 3076
  7.3 18.5 %copy-start = (bf16[256,512]{1,0:T(8,128)(2,1)S(1)}, bf16[256,512]{1,0:T(8,128)(2,1)}, u32[]{:S(2)}) copy-start(bf16[256,512]{1,0:T(8,128)(2,1)} %param.10) | copy-start | bytes 786436
  7.3 154.7 %all-gather.5.cloned.1.call-start = ((), (), s32[]{:S(2)}) async-start(), calls=%async_computation.1 | async-start | bytes 17825792 | tf_op jit(solution)/shard_map/all_gather | solution.py:56
Sparse Core Ops, SparseCore 0:
  8.9 23.9 all-gather.2
  35.1 126.8 all-gather.4
where the time goes:
time: 247 us; the launch traced here: 246 us
  waiting for transfers between devices  134 us (54%)
  matrix products  87.4 us (35%)
  between operations  14.1 us (6%)
  blocking collectives  5.01 us (2%)
  other arithmetic  2.5 us (1%)
    all_gather x1, waiting for transfers between devices, body(): gathered = lax.all_gather(dressed, 'pair', axis=0, tiled=True)  127 us
    dot_general x32, matrix products, ladder_block(): jnp.einsum('pqad,qbd->pab', half_done, slab_block, preferred_element_type...  70.4 us
    dot_general x1, matrix products, body(): jnp.einsum('ka,qkc->qac', dressing_cols, occ_slabs, preferred_element_typ...  16.6 us
    all_gather x1, waiting for transfers between devices, body(): full_doubles = lax.all_gather(doubles, 'aux', axis=1, tiled=True)  6.74 us
    unnamed x1, blocking collectives  5.01 us
  transfers between devices with their start and end apart: 2, of which 2 were waited for; matrix products, arithmetic and copies ran while one was open for 8% of the time, Pallas kernels for 0%

commit v1 on v0

v1 whole, which is shorter than its diff:
```python
import functools
import math

import jax
import jax.numpy as jnp
from jax import lax
from jax.experimental import pallas as pl
from jax.experimental.pallas import tpu as pltpu
from jax.sharding import PartitionSpec as P

MESH = pl.DeviceIdType.MESH


def inner_group(n_pair):
    size = 2
    while size * size < n_pair:
        size *= 2
    return math.gcd(size, n_pair)


def ladder_kernel(
    n_pair, n_aux, group, win,
    tau_ref, lhs_ref, vir_ref, tile_ref, occ_ref,
    out_ref, tile_out_ref,
    tau, dressed, slabs, half_buf, total, fold, parts, tiles,
    own_sem, slab_sem, z_send, z_recv, y_send, y_recv,
    x_send, x_recv, c_send, c_recv, r_send, r_recv, t_send, t_recv,
):
    lines = n_pair // group
    cols = group // 2
    per_dev, rows_c, width = tau_ref.shape
    rows = vir_ref.shape[0]
    sends = x_recv.shape[1]
    send_rows = rows // sends
    slab_rows = slabs.shape[1]
    depth = lhs_ref.shape[1]
    steps = occ_ref.shape[0] // slab_rows
    step_rows = rows // steps
    block = total.shape[1]

    pair = lax.axis_index("pair")
    aux = lax.axis_index("aux")
    z = pair // group
    g = pair % group
    col = g // 2
    core = g % 2

    def at(zz, gg, aa):
        return {"pair": zz * group + gg, "aux": aa}

    def slab_copy(step):
        slot = lax.rem(step, slabs.shape[0])
        return pltpu.make_async_copy(
            occ_ref.at[pl.ds(step * slab_rows, slab_rows)], slabs.at[slot], slab_sem.at[slot]
        )

    depth_slots = slabs.shape[0]
    for step in range(min(depth_slots, steps)):
        slab_copy(step).start()
    own_rows = pl.ds(pl.multiple_of(aux * rows_c, rows_c), rows_c)
    own = pltpu.make_async_copy(tau_ref, tau.at[z, :, own_rows], own_sem)
    own.start()
    tiles[aux] = tile_ref[...]

    barrier = pltpu.get_barrier_semaphore()
    for dz in range(lines):
        for da in range(n_aux):
            if dz or da:
                pl.semaphore_signal(
                    barrier, inc=1, device_id=at((z + dz) % lines, g, (aux + da) % n_aux), device_id_type=MESH
                )
    for dg in range(1, group):
        pl.semaphore_signal(barrier, inc=1, device_id=at(z, (g + dg) % group, aux), device_id_type=MESH)
    pl.semaphore_wait(barrier, lines * n_aux - 1 + group - 1)
    own.wait()

    def piece(zz, k, aa):
        return tau.at[zz, k, pl.ds(pl.multiple_of(aa * rows_c, rows_c), rows_c)]

    def z_copy(zz, k, way):
        ref = piece(zz, k, aux)
        return pltpu.make_async_remote_copy(
            src_ref=ref, dst_ref=ref, send_sem=z_send.at[(way + 1) // 2, zz, k],
            recv_sem=z_recv.at[zz, k], device_id=at(z + way, g, aux), device_id_type=MESH,
        )

    def y_copy(zz, k, aa, other):
        ref = piece(zz, k, aa)
        return pltpu.make_async_remote_copy(
            src_ref=ref, dst_ref=ref, send_sem=y_send.at[zz, k, other],
            recv_sem=y_recv.at[zz, k, aa], device_id=at(z, g, other), device_id_type=MESH,
        )

    def onward(zz, k, ways):
        for way in ways:
            @pl.when((z + way >= 0) & (z + way < lines))
            def _():
                z_copy(zz, k, way).start()
        for da in range(1, n_aux):
            y_copy(zz, k, aux, (aux + da) % n_aux).start()

    def relay(dist, k):
        for way in (-1, 1):
            source = z - way * dist

            @pl.when((source >= 0) & (source < lines))
            def _():
                z_copy(source, k, way).wait_recv()
                onward(source, k, (way,))

    def x_copy(owner_col, part, to_col):
        ref = dressed.at[owner_col * 2 + core, pl.ds(part * send_rows, send_rows)]
        return pltpu.make_async_remote_copy(
            src_ref=ref, dst_ref=ref, send_sem=x_send.at[to_col, part],
            recv_sem=x_recv.at[owner_col, part], device_id=at(z, to_col * 2 + core, aux), device_id_type=MESH,
        )

    def c_copy(owner_col, owner_core, part):
        ref = dressed.at[owner_col * 2 + owner_core, pl.ds(part * send_rows, send_rows)]
        return pltpu.make_async_remote_copy(
            src_ref=ref, dst_ref=ref, send_sem=c_send.at[owner_col, part],
            recv_sem=c_recv.at[owner_col, part], device_id=at(z, col * 2 + 1 - core, aux), device_id_type=MESH,
        )

    def tile_copy(source, other):
        return pltpu.make_async_remote_copy(
            src_ref=tiles.at[source], dst_ref=tiles.at[source], send_sem=t_send.at[other],
            recv_sem=t_recv.at[source], device_id=at(z, g, other), device_id_type=MESH,
        )

    def other_cols():
        return [(col + dc) % cols for dc in range(1, cols)]

    def pass_block(part):
        for owner in other_cols():
            x_copy(owner, part, owner).wait_recv()
            c_copy(owner, core, part).start()

    for k in range(per_dev):
        onward(z, k, (-1, 1))
    for da in range(1, n_aux):
        tile_copy(aux, (aux + da) % n_aux).start()

    def dress(step, carry):
        slab_copy(step).wait()
        slot = lax.rem(step, depth_slots)
        for i in range(slab_rows // depth):
            acc = jnp.dot(
                lhs_ref[...], slabs[slot, i * depth:(i + 1) * depth, :], preferred_element_type=jnp.float32
            )
            start = pl.multiple_of(step * step_rows + i * 2 * win, 2 * win)
            made = vir_ref[pl.ds(start, 2 * win), :].astype(jnp.float32) - acc
            dressed[g, pl.ds(start, 2 * win), :] = made.astype(jnp.bfloat16)

        @pl.when(step + depth_slots < steps)
        def _():
            slab_copy(step + depth_slots).start()
        return carry

    events = {}
    if lines > 1:
        for k in range(per_dev):
            when = min(steps, max(1, (steps * (7 + 5 * k)) // 16))
            events.setdefault(when, []).append(functools.partial(relay, 1, k))
    passed = 0
    for part in range(sends):
        made_at = (part + 1) * steps // sends

        def send_own(part=part):
            for to_col in other_cols():
                x_copy(col, part, to_col).start()
            c_copy(col, core, part).start()

        events.setdefault(made_at, []).append(send_own)
        if part * 2 < sends:
            later = (part + 1) * steps // sends + (6 * steps) // 16
            if later < steps:
                events.setdefault(later, []).append(functools.partial(pass_block, part))
                passed = part + 1
    begin = 0
    for stop in sorted(events):
        if stop > begin:
            lax.fori_loop(begin, stop, dress, 0)
            begin = stop
        for action in events[stop]:
            action()
    if begin < steps:
        lax.fori_loop(begin, steps, dress, 0)

    total[...] = jnp.zeros_like(total)

    def unit(zz, k, gg):
        half_buf[...] = jnp.dot(
            dressed[gg], tau[zz, k], preferred_element_type=jnp.float32
        ).astype(jnp.bfloat16)
        acc = None
        for i in range(rows // block):
            term = lax.dot_general(
                half_buf[i * block:(i + 1) * block, :],
                dressed[gg, pl.ds(i * block, block), :],
                (((1,), (1,)), ((), ())), preferred_element_type=jnp.float32,
            )
            acc = term if acc is None else acc + term
        total[zz * per_dev + k] += acc

    def nth_group(i):
        return ((col + i // 2) % cols) * 2 + (core + i % 2) % 2

    def units(zz, k, first, last):
        def one(i, carry):
            unit(zz, k, nth_group(i))
            return carry

        lax.fori_loop(first, last, one, 0)

    def nth_line(t):
        near = jnp.minimum(z, lines - 1 - z)
        side = (t + 1) // 2 * (1 - 2 * (t % 2))
        rest = jnp.where(z + z <= lines - 1, t, lines - 1 - t)
        return jnp.where(t <= 2 * near, z + side, rest)

    def arrived(zz, k):
        for da in range(1, n_aux):
            source = (aux + da) % n_aux
            y_copy(zz, k, source, source).wait_recv()

    for k in range(per_dev):
        if lines > 2:
            relay(2, k)
        arrived(z, k)
        units(z, k, 0, 1)
        if k == 0:
            for part in range(sends):
                c_copy(col, 1 - core, part).wait_recv()
        units(z, k, 1, 2)
        for part in range(passed, min(sends, passed + 1)):
            pass_block(part)
            passed = part + 1
    for part in range(passed, sends):
        pass_block(part)
    for owner in other_cols():
        for part in range(sends):
            c_copy(owner, 1 - core, part).wait_recv()
    for k in range(per_dev):
        if lines > 3:
            relay(3, k)
        units(z, k, 2, group)
    for t in range(1, lines):
        zz = nth_line(t)
        for k in range(per_dev):
            if t + 3 < lines:
                relay(t + 3, k)
            arrived(zz, k)
            units(zz, k, 0, group)

    down = lax.broadcasted_iota(jnp.int32, (block, block), 0) // win
    across = lax.broadcasted_iota(jnp.int32, (block, block), 1) // win
    on_diagonal = down == across
    for zz in range(lines):
        for k in range(per_dev):
            kept = jnp.where(on_diagonal, total[zz * per_dev + k], 0.0)
            fold[zz, k] = jnp.sum(kept.reshape(block // win, win, block), axis=0)

    def sum_copy(source_z, source_aux, to_z, to_aux):
        return pltpu.make_async_remote_copy(
            src_ref=fold.at[to_z], dst_ref=parts.at[source_z, source_aux],
            send_sem=r_send.at[to_z, to_aux], recv_sem=r_recv.at[source_z, source_aux],
            device_id=at(to_z, g, to_aux), device_id_type=MESH,
        )

    others = [
        ((z + dz) % lines, (aux + da) % n_aux)
        for dz in range(lines) for da in range(n_aux) if dz or da
    ]
    for to_z, to_aux in others:
        sum_copy(z, aux, to_z, to_aux).start()
    parts[z, aux] = fold[z]
    for from_z, from_aux in others:
        sum_copy(from_z, from_aux, from_z, from_aux).wait_recv()
    result = parts[0, 0]
    for i in range(1, lines * n_aux):
        result = result + parts[i // n_aux, i % n_aux]
    out_ref[...] = result
    for da in range(1, n_aux):
        source = (aux + da) % n_aux
        tile_copy(source, source).wait_recv()
    tile_out_ref[...] = tiles[0]

    for to_z, to_aux in others:
        sum_copy(z, aux, to_z, to_aux).wait_send()
    for da in range(1, n_aux):
        tile_copy(aux, (aux + da) % n_aux).wait_send()
    for part in range(sends):
        for to_col in other_cols():
            x_copy(col, part, to_col).wait_send()
        for dc in range(cols):
            c_copy((col + dc) % cols, core, part).wait_send()
    for k in range(per_dev):
        for zz in range(lines):
            for da in range(1, n_aux):
                y_copy(zz, k, aux, (aux + da) % n_aux).wait_send()

            @pl.when((zz <= z) & (z + 1 < lines))
            def _():
                z_copy(zz, k, 1).wait_send()

            @pl.when((zz >= z) & (z >= 1))
            def _():
                z_copy(zz, k, -1).wait_send()


def body(n_pair, n_aux, doubles, singles, vir_slabs, occ_slabs, occ_energy, vir_energy, pair_list):
    per_dev, rows_c, width = doubles.shape
    aux_count, win, _ = vir_slabs.shape
    occ_count = singles.shape[0]
    group = inner_group(n_pair)
    lines = n_pair // group
    cols = group // 2
    aux = lax.axis_index("aux")

    occ_ids = lax.broadcasted_iota(jnp.int32, (per_dev, occ_count), 1)
    match_first = pair_list[:, 0][:, None] == occ_ids
    match_second = pair_list[:, 1][:, None] == occ_ids
    row_first = jnp.dot(match_first.astype(jnp.bfloat16), singles, preferred_element_type=jnp.float32)
    row_second = jnp.dot(match_second.astype(jnp.bfloat16), singles, preferred_element_type=jnp.float32)
    own_first = lax.dynamic_slice_in_dim(row_first, aux * rows_c, rows_c, 1)
    tau_own = (
        doubles.astype(jnp.float32) + own_first[:, :, None] * row_second[:, None, :]
    ).astype(jnp.bfloat16)

    dressing = singles[:, :win].T
    blank = jnp.zeros_like(dressing)
    lhs = jnp.concatenate(
        [jnp.concatenate([dressing, blank], axis=1), jnp.concatenate([blank, dressing], axis=1)], axis=0
    )
    rows = aux_count * win
    block = math.gcd(rows, 256)
    chunk = math.gcd(aux_count, 8)
    steps = aux_count // chunk
    sends = math.gcd(steps, 4)
    slots = min(3, steps)
    tile_rows = max(16, win)
    tile = doubles[:, :tile_rows, :128]

    dma = pltpu.SemaphoreType.DMA
    vmem = pl.BlockSpec(memory_space=pltpu.VMEM)
    anywhere = pl.BlockSpec(memory_space=pl.ANY)
    pieces, tiles = pl.pallas_call(
        functools.partial(ladder_kernel, n_pair, n_aux, group, win),
        out_shape=(
            jax.ShapeDtypeStruct((per_dev, win, block), jnp.float32),
            jax.ShapeDtypeStruct(tile.shape, tile.dtype),
        ),
        in_specs=[anywhere, vmem, vmem, vmem, anywhere],
        out_specs=(vmem, vmem),
        scratch_shapes=[
            pltpu.VMEM((lines, per_dev, width, width), jnp.bfloat16),
            pltpu.VMEM((group, rows, width), jnp.bfloat16),
            pltpu.VMEM((slots, chunk * occ_count, width), jnp.bfloat16),
            pltpu.VMEM((rows, width), jnp.bfloat16),
            pltpu.VMEM((lines * per_dev, block, block), jnp.float32),
            pltpu.VMEM((lines, per_dev, win, block), jnp.float32),
            pltpu.VMEM((lines, n_aux, per_dev, win, block), jnp.float32),
            pltpu.VMEM((n_aux,) + tile.shape, tile.dtype),
            dma, dma((slots,)),
            dma((2, lines, per_dev)), dma((lines, per_dev)),
            dma((lines, per_dev, n_aux)), dma((lines, per_dev, n_aux)),
            dma((cols, sends)), dma((cols, sends)),
            dma((cols, sends)), dma((cols, sends)),
            dma((lines, n_aux)), dma((lines, n_aux)),
            dma((n_aux,)), dma((n_aux,)),
        ],
        compiler_params=pltpu.CompilerParams(
            collective_id=0, has_side_effects=True, vmem_limit_bytes=50 * 1024 * 1024
        ),
        cost_estimate=pl.CostEstimate(
            flops=2 * lines * per_dev * group * rows * width * (width + block),
            bytes_accessed=2 * occ_slabs.size, transcendentals=0,
        ),
    )(tau_own, lhs, vir_slabs.reshape(rows, width), tile, occ_slabs.reshape(aux_count * occ_count, width))

    residual = jnp.sum(pieces.reshape(per_dev, win, block // win, win), axis=2)
    share_rows = win // n_aux
    row_start = aux * share_rows
    share = lax.dynamic_slice_in_dim(residual, row_start, share_rows, 1)
    own_doubles = lax.dynamic_slice_in_dim(tiles[:, :win, :win], row_start, share_rows, 1)
    own_vir = lax.dynamic_slice_in_dim(vir_energy, row_start, share_rows, 0)
    energy_first = jnp.sum(jnp.where(match_first, occ_energy[None, :], 0.0), axis=1)
    energy_second = jnp.sum(jnp.where(match_second, occ_energy[None, :], 0.0), axis=1)
    pair_energy = energy_first + energy_second
    denominator = pair_energy[:, None, None] - own_vir[None, :, None] - vir_energy[None, None, :]
    return own_doubles.astype(jnp.float32) + share / denominator


def solution(mesh):
    placed = (
        P("pair", "aux", None),
        P(),
        P(("aux", "pair"), None, None),
        P(("aux", "pair"), None, None),
        P(),
        P(),
        P("pair", None),
    )
    return jax.shard_map(
        functools.partial(body, mesh.shape["pair"], mesh.shape["aux"]),
        mesh=mesh, in_specs=placed, out_specs=P("pair", "aux", None), check_vma=False,
    )
```

time: 247 us -> 91.9 us (0.37)
  waiting for transfers between devices: 134 us -> 0 us
  matrix products: 87.4 us -> 2.27 us
  Pallas kernels: 0 us -> 81.5 us
  between operations: 14.1 us -> 0.07 us
  blocking collectives: 5.01 us -> 0 us
  local copies, waits for them, and re-layouts: 1.57 us -> 4.69 us
    all_gather x2 -> x0, waiting for transfers between devices: 134 us -> none  [the longest x1 127 us: body(): gathered = lax.all_gather(dressed, 'pair', axis=0, tiled=True)]
    dot_general x33 -> x0, matrix products: 87 us -> none  [the longest x32 70.4 us: ladder_block(): jnp.einsum('pqad,qbd->pab', half_done, slab_block, preferred_element_type...]
    pallas_call x0 -> x1, Pallas kernels: none -> 81.5 us  [body(): pl.pallas_call(functools.partial(ladder_kernel, n_pair, n_aux, group, win...]
    unnamed x1 -> x0, blocking collectives: 5.01 us -> none
  transfers between devices with their start and end apart: 2 -> 0, of which waited for: 2 -> 0; matrix products, arithmetic and copies ran while one was open for 8% -> 0% of each run, Pallas kernels for 0% -> 0%
where the time goes in v1:
time: 91.9 us; the launch traced here: 91.5 us
  Pallas kernels  81.5 us (89%)
  local copies, waits for them, and re-layouts  4.69 us (5%)
  other arithmetic  2.95 us (3%)
  matrix products  2.27 us (2%)
    pallas_call x1, Pallas kernels, body(): pl.pallas_call(functools.partial(ladder_kernel, n_pair, n_aux, group, win...  81.5 us

profile of v1, /device:TPU:0, one launch (start us, length us, event | category | flops | bytes accessed | tf_op | source)
XLA Modules:
  0.0 91.5 jit_solution(6456135260037394147)
XLA Ops:
  0.0 0.7 dynamic_slice.15
  0.7 1.0 %slice_reduce_fusion.1 = (s32[2]{0:T(128)S(1)}, s32[2]{0:T(128)S(1)}) fusion(s32[2,2]{1,0:T(2,128)} %param.13), kind=kLoop, calls=%fused_computation.16 | loop fusion | bytes 32 | tf_op jit(solution)/shard_map/slice | solution.py:322
  1.7 0.9 select_reduce_fusion
  2.6 0.1 broadcast_subtract_fusion
  2.7 1.1 %fusion.4 = f32[2,512]{1,0:T(2,128)S(1)} fusion(bf16[256,512]{1,0:T(8,128)(2,1)} %param.8, s32[2]{0:T(128)S(1)} %get-tuple-element.11), kind=kOutput, calls=%fused_computation.12 | convolution fusion | flops 524800 | bytes 266248 | tf_op jit(solution)/shard_map/dot_general | solution.py:324
  3.8 1.1 %fusion.3 = f32[2,512]{1,0:T(2,128)S(1)} fusion(bf16[256,512]{1,0:T(8,128)(2,1)} %param.8, s32[2]{0:T(128)S(1)} %get-tuple-element.12), kind=kOutput, calls=%fused_computation.10 | convolution fusion | flops 524800 | bytes 266248 | tf_op jit(solution)/shard_map/dot_general | solution.py:325
  5.0 0.7 slice.18.tile_ref
  5.7 0.8 slice.17
  6.5 0.1 copy.11
  6.6 1.2 %add_convert_fusion.tau_ref = bf16[2,256,512]{2,1,0:T(8,128)(2,1)S(1)} fusion(bf16[2,256,512]{2,1,0:T(8,128)(2,1)} %param.7, f32[2,512]{1,0:T(2,128)S(1)} %fusion.3, f32[2,256]{1,0:T(2,128)S(1)} %constant_dynamic-slice_fusion), kind=kLoop, calls=%fused_computation | loop fusion | flops 1048576 | bytes 1054720 | tf_op jit(solution)/shard_map/convert_element_type | solution.py:329
  7.8 0.0 copy-start
  7.8 1.2 %copy-done = bf16[128,8,512]{2,1,0:T(8,128)(2,1)S(1)} copy-done((bf16[128,8,512]{2,1,0:T(8,128)(2,1)S(1)}, bf16[128,8,512]{2,1,0:T(8,128)(2,1)}, u32[]{:S(2)}) %copy-start) | copy-done | bytes 1048600
  9.1 0.0 copy-start.1
  9.1 81.5 %shard_map.73 = (f32[2,8,256]{2,1,0:T(8,128)S(1)}, bf16[2,16,128]{2,1,0:T(8,128)(2,1)S(1)}) custom-call(bf16[2,256,512]{2,1,0:T(8,128)(2,1)S(1)} %add_convert_fusion.tau_ref, bf16[16,512]{1,0:T(8,128)(2,1)S(1)} %fusion.2.lhs_ref, bf16[1024,512]{1,0:T(8,128)(2,1)S(1)} %bitcast.5, bf16[2,16,128]{2,1,0:T(8,128)(2,1)S(1)} %slice.18.tile_ref, ...), custom_call_target="tpu_custom_call" | custom-call | flops 25769803776 | bytes 33554432 | tf_op jit(solution)/shard_map/pallas_call | solution.py:348
  90.6 0.2 reshape.51
  90.8 0.0 copy-done.1
  90.8 0.7 divide_add_fusion
  (5 shorter events, 0.1 us)
Async XLA Ops:
  7.8 1.2 %copy-start = (bf16[128,8,512]{2,1,0:T(8,128)(2,1)S(1)}, bf16[128,8,512]{2,1,0:T(8,128)(2,1)}, u32[]{:S(2)}) copy-start(bf16[128,8,512]{2,1,0:T(8,128)(2,1)} %param.9) | copy-start | bytes 3145732
  9.1 81.8 %copy-start.1 = (f32[8]{0:T(128)S(1)}, f32[8]{0:T(128)}, u32[]{:S(2)}) copy-start(f32[8]{0:T(128)} %param.12) | copy-start | bytes 100

commit v2 on v1

--- a/solution.py
+++ b/solution.py
@@ -20,20 +20,23 @@
 
 def ladder_kernel(
     n_pair, n_aux, group, win,
-    tau_ref, lhs_ref, vir_ref, tile_ref, occ_ref,
-    out_ref, tile_out_ref,
-    tau, dressed, slabs, half_buf, total, fold, parts, tiles,
-    own_sem, slab_sem, z_send, z_recv, y_send, y_recv,
+    pair_ref, energy_ref, doubles_ref, singles_ref, vir_hbm, occ_ref,
+    out_ref, tile_out_ref, energy_out_ref,
+    tau, dressed, slabs, total, fold, parts, tiles, own_ref, vir_ref, outer, lhs_ref,
+    own_sem, vir_sem, slab_sem, z2_send, z2_recv, y2_send, y2_recv, z_send, z_recv, y_send, y_recv,
     x_send, x_recv, c_send, c_recv, r_send, r_recv, t_send, t_recv,
 ):
     lines = n_pair // group
     cols = group // 2
-    per_dev, rows_c, width = tau_ref.shape
+    per_dev, rows_c, width = doubles_ref.shape
     rows = vir_ref.shape[0]
     sends = x_recv.shape[1]
     send_rows = rows // sends
     slab_rows = slabs.shape[1]
+    occ_count = singles_ref.shape[0]
     depth = lhs_ref.shape[1]
+    tile_rows, tile_cols = tiles.shape[2:]
+    extra = rows_c // 4 if n_aux > 1 and rows_c % 64 == 0 else 0
     steps = occ_ref.shape[0] // slab_rows
     step_rows = rows // steps
     block = total.shape[1]
@@ -58,9 +61,10 @@
     for step in range(min(depth_slots, steps)):
         slab_copy(step).start()
     own_rows = pl.ds(pl.multiple_of(aux * rows_c, rows_c), rows_c)
-    own = pltpu.make_async_copy(tau_ref, tau.at[z, :, own_rows], own_sem)
+    own = pltpu.make_async_copy(doubles_ref, own_ref, own_sem)
     own.start()
-    tiles[aux] = tile_ref[...]
+    vir_copy = pltpu.make_async_copy(vir_hbm, vir_ref, vir_sem)
+    vir_copy.start()
 
     barrier = pltpu.get_barrier_semaphore()
     for dz in range(lines):
@@ -74,8 +78,64 @@
     pl.semaphore_wait(barrier, lines * n_aux - 1 + group - 1)
     own.wait()
 
+    pick = lax.broadcasted_iota(jnp.int32, (16, occ_count), 1)
+    top = lax.broadcasted_iota(jnp.int32, (16, occ_count), 0) == 0
+
+    def picked(index):
+        one_hot = jnp.where(top & (pick == index), 1.0, 0.0).astype(jnp.bfloat16)
+        return jnp.dot(one_hot, singles_ref[...], preferred_element_type=jnp.float32).astype(jnp.bfloat16)
+
+    for k in range(per_dev):
+        outer[...] = lax.dot_general(
+            picked(pair_ref[k, 0]), picked(pair_ref[k, 1]), (((0,), (0,)), ((), ())),
+            preferred_element_type=jnp.float32,
+        )
+        tau[z, k, own_rows] = (own_ref[k].astype(jnp.float32) + outer[own_rows, :]).astype(jnp.bfloat16)
+
     def piece(zz, k, aa):
-        return tau.at[zz, k, pl.ds(pl.multiple_of(aa * rows_c, rows_c), rows_c)]
+        count = rows_c - extra if k == per_dev - 1 else rows_c
+        return tau.at[zz, k, pl.ds(pl.multiple_of(aa * rows_c, rows_c), count)]
+
+    def last_rows(zz, aa):
+        start = pl.multiple_of(aa * rows_c + rows_c - extra, 16)
+        return tau.at[zz, per_dev - 1, pl.ds(start, extra)]
+
+    def z2_copy(zz, aa, way):
+        ref = last_rows(zz, aa)
+        return pltpu.make_async_remote_copy(
+            src_ref=ref, dst_ref=ref, send_sem=z2_send.at[(way + 1) // 2, zz, aa],
+            recv_sem=z2_recv.at[zz, aa], device_id=at(z + way, g, aux), device_id_type=MESH,
+        )
+
+    def y2_copy(aa, other):
+        ref = last_rows(z, aa)
+        return pltpu.make_async_remote_copy(
+            src_ref=ref, dst_ref=ref, send_sem=y2_send.at[other],
+            recv_sem=y2_recv.at[aa], device_id=at(z, g, other), device_id_type=MESH,
+        )
+
+    def onward2(zz, aa, ways):
+        for way in ways:
+            @pl.when((z + way >= 0) & (z + way < lines))
+            def _():
+                z2_copy(zz, aa, way).start()
+
+    def spread2():
+        for da in range(1, n_aux):
+            source = (aux + da) % n_aux
+            y2_copy(source, source).wait_recv()
+            onward2(z, source, (-1, 1))
+
+    def relay2(dist):
+        for way in (-1, 1):
+            source = z - way * dist
+
+            @pl.when((source >= 0) & (source < lines))
+            def _():
+                for da in range(n_aux):
+                    aa = (aux + da) % n_aux
+                    z2_copy(source, aa, way).wait_recv()
+                    onward2(source, aa, (way,))
 
     def z_copy(zz, k, way):
         ref = piece(zz, k, aux)
@@ -107,6 +167,9 @@
             def _():
                 z_copy(source, k, way).wait_recv()
                 onward(source, k, (way,))
+
+        if extra and k == per_dev - 1:
+            relay2(dist)
 
     def x_copy(owner_col, part, to_col):
         ref = dressed.at[owner_col * 2 + core, pl.ds(part * send_rows, send_rows)]
@@ -136,10 +199,26 @@
             x_copy(owner, part, owner).wait_recv()
             c_copy(owner, core, part).start()
 
+    if extra:
+        for da in range(1, n_aux):
+            y2_copy(aux, (aux + da) % n_aux).start()
     for k in range(per_dev):
         onward(z, k, (-1, 1))
+    if extra:
+        onward2(z, aux, (-1, 1))
+    tiles[aux] = own_ref[:, :tile_rows, :tile_cols]
     for da in range(1, n_aux):
         tile_copy(aux, (aux + da) % n_aux).start()
+
+    across = lax.broadcasted_iota(jnp.int32, (2 * win, width), 1)
+    down = lax.broadcasted_iota(jnp.int32, (2 * win, width), 0)
+    for half in range(2):
+        chosen = (down // win == half) & (across == down - half * win)
+        lhs_ref[:, half * occ_count:(half + 1) * occ_count] = lax.dot_general(
+            jnp.where(chosen, 1.0, 0.0).astype(jnp.bfloat16), singles_ref[...],
+            (((1,), (1,)), ((), ())), preferred_element_type=jnp.float32,
+        ).astype(jnp.bfloat16)
+    vir_copy.wait()
 
     def dress(step, carry):
         slab_copy(step).wait()
@@ -158,6 +237,8 @@
         return carry
 
     events = {}
+    if extra:
+        events.setdefault(min(steps, max(1, steps // 5)), []).append(spread2)
     if lines > 1:
         for k in range(per_dev):
             when = min(steps, max(1, (steps * (7 + 5 * k)) // 16))
@@ -190,15 +271,12 @@
     total[...] = jnp.zeros_like(total)
 
     def unit(zz, k, gg):
-        half_buf[...] = jnp.dot(
-            dressed[gg], tau[zz, k], preferred_element_type=jnp.float32
-        ).astype(jnp.bfloat16)
         acc = None
         for i in range(rows // block):
+            slab = dressed[gg, pl.ds(i * block, block), :]
+            half = jnp.dot(slab, tau[zz, k], preferred_element_type=jnp.float32).astype(jnp.bfloat16)
             term = lax.dot_general(
-                half_buf[i * block:(i + 1) * block, :],
-                dressed[gg, pl.ds(i * block, block), :],
-                (((1,), (1,)), ((), ())), preferred_element_type=jnp.float32,
+                half, slab, (((1,), (1,)), ((), ())), preferred_element_type=jnp.float32
             )
             acc = term if acc is None else acc + term
         total[zz * per_dev + k] += acc
@@ -285,6 +363,10 @@
         source = (aux + da) % n_aux
         tile_copy(source, source).wait_recv()
     tile_out_ref[...] = tiles[0]
+    for k in range(per_dev):
+        energy_out_ref[k] = jnp.full(
+            energy_out_ref.shape[1:], energy_ref[pair_ref[k, 0]] + energy_ref[pair_ref[k, 1]], jnp.float32
+        )
 
     for to_z, to_aux in others:
         sum_copy(z, aux, to_z, to_aux).wait_send()
@@ -295,6 +377,19 @@
             x_copy(col, part, to_col).wait_send()
         for dc in range(cols):
             c_copy((col + dc) % cols, core, part).wait_send()
+    if extra:
+        for da in range(1, n_aux):
+            y2_copy(aux, (aux + da) % n_aux).wait_send()
+        for zz in range(lines):
+            @pl.when((zz <= z) & (z + 1 < lines))
+            def _():
+                for aa in range(n_aux):
+                    z2_copy(zz, aa, 1).wait_send()
+
+            @pl.when((zz >= z) & (z >= 1))
+            def _():
+                for aa in range(n_aux):
+                    z2_copy(zz, aa, -1).wait_send()
     for k in range(per_dev):
         for zz in range(lines):
             for da in range(1, n_aux):
@@ -318,51 +413,42 @@
     cols = group // 2
     aux = lax.axis_index("aux")
 
-    occ_ids = lax.broadcasted_iota(jnp.int32, (per_dev, occ_count), 1)
-    match_first = pair_list[:, 0][:, None] == occ_ids
-    match_second = pair_list[:, 1][:, None] == occ_ids
-    row_first = jnp.dot(match_first.astype(jnp.bfloat16), singles, preferred_element_type=jnp.float32)
-    row_second = jnp.dot(match_second.astype(jnp.bfloat16), singles, preferred_element_type=jnp.float32)
-    own_first = lax.dynamic_slice_in_dim(row_first, aux * rows_c, rows_c, 1)
-    tau_own = (
-        doubles.astype(jnp.float32) + own_first[:, :, None] * row_second[:, None, :]
-    ).astype(jnp.bfloat16)
-
-    dressing = singles[:, :win].T
-    blank = jnp.zeros_like(dressing)
-    lhs = jnp.concatenate(
-        [jnp.concatenate([dressing, blank], axis=1), jnp.concatenate([blank, dressing], axis=1)], axis=0
-    )
     rows = aux_count * win
     block = math.gcd(rows, 256)
     chunk = math.gcd(aux_count, 8)
     steps = aux_count // chunk
     sends = math.gcd(steps, 4)
-    slots = min(3, steps)
+    slots = min(6, steps)
     tile_rows = max(16, win)
-    tile = doubles[:, :tile_rows, :128]
+    tile_shape = (per_dev, tile_rows, min(width, 128))
 
     dma = pltpu.SemaphoreType.DMA
     vmem = pl.BlockSpec(memory_space=pltpu.VMEM)
+    smem = pl.BlockSpec(memory_space=pltpu.SMEM)
     anywhere = pl.BlockSpec(memory_space=pl.ANY)
-    pieces, tiles = pl.pallas_call(
+    pieces, tiles, energies = pl.pallas_call(
         functools.partial(ladder_kernel, n_pair, n_aux, group, win),
         out_shape=(
             jax.ShapeDtypeStruct((per_dev, win, block), jnp.float32),
-            jax.ShapeDtypeStruct(tile.shape, tile.dtype),
+            jax.ShapeDtypeStruct(tile_shape, doubles.dtype),
+            jax.ShapeDtypeStruct((per_dev, 8, 128), jnp.float32),
         ),
-        in_specs=[anywhere, vmem, vmem, vmem, anywhere],
-        out_specs=(vmem, vmem),
+        in_specs=[smem, smem, anywhere, vmem, anywhere, anywhere],
+        out_specs=(vmem, vmem, vmem),
         scratch_shapes=[
             pltpu.VMEM((lines, per_dev, width, width), jnp.bfloat16),
             pltpu.VMEM((group, rows, width), jnp.bfloat16),
             pltpu.VMEM((slots, chunk * occ_count, width), jnp.bfloat16),
-            pltpu.VMEM((rows, width), jnp.bfloat16),
             pltpu.VMEM((lines * per_dev, block, block), jnp.float32),
             pltpu.VMEM((lines, per_dev, win, block), jnp.float32),
             pltpu.VMEM((lines, n_aux, per_dev, win, block), jnp.float32),
-            pltpu.VMEM((n_aux,) + tile.shape, tile.dtype),
-            dma, dma((slots,)),
+            pltpu.VMEM((n_aux,) + tile_shape, doubles.dtype),
+            pltpu.VMEM(doubles.shape, doubles.dtype),
+            pltpu.VMEM((rows, width), jnp.bfloat16),
+            pltpu.VMEM((width, width), jnp.float32),
+            pltpu.VMEM((2 * win, 2 * occ_count), jnp.bfloat16),
+            dma, dma, dma((slots,)),
+            dma((2, lines, n_aux)), dma((lines, n_aux)), dma((n_aux,)), dma((n_aux,)),
             dma((2, lines, per_dev)), dma((lines, per_dev)),
             dma((lines, per_dev, n_aux)), dma((lines, per_dev, n_aux)),
             dma((cols, sends)), dma((cols, sends)),
@@ -371,13 +457,16 @@
             dma((n_aux,)), dma((n_aux,)),
         ],
         compiler_params=pltpu.CompilerParams(
-            collective_id=0, has_side_effects=True, vmem_limit_bytes=50 * 1024 * 1024
+            collective_id=0, has_side_effects=True, vmem_limit_bytes=56 * 1024 * 1024
         ),
         cost_estimate=pl.CostEstimate(
             flops=2 * lines * per_dev * group * rows * width * (width + block),
             bytes_accessed=2 * occ_slabs.size, transcendentals=0,
         ),
-    )(tau_own, lhs, vir_slabs.reshape(rows, width), tile, occ_slabs.reshape(aux_count * occ_count, width))
+    )(
+        pair_list, occ_energy, doubles, singles, vir_slabs.reshape(rows, width),
+        occ_slabs.reshape(aux_count * occ_count, width),
+    )
 
     residual = jnp.sum(pieces.reshape(per_dev, win, block // win, win), axis=2)
     share_rows = win // n_aux
@@ -385,9 +474,7 @@
     share = lax.dynamic_slice_in_dim(residual, row_start, share_rows, 1)
     own_doubles = lax.dynamic_slice_in_dim(tiles[:, :win, :win], row_start, share_rows, 1)
     own_vir = lax.dynamic_slice_in_dim(vir_energy, row_start, share_rows, 0)
-    energy_first = jnp.sum(jnp.where(match_first, occ_energy[None, :], 0.0), axis=1)
-    energy_second = jnp.sum(jnp.where(match_second, occ_energy[None, :], 0.0), axis=1)
-    pair_energy = energy_first + energy_second
+    pair_energy = energies[:, 0, 0]
     denominator = pair_energy[:, None, None] - own_vir[None, :, None] - vir_energy[None, None, :]
     return own_doubles.astype(jnp.float32) + share / denominator
 

time: 91.9 us -> 92.4 us (level)
  Pallas kernels: 81.5 us -> 88.2 us
  matrix products: 2.27 us -> 0 us
  other arithmetic: 2.95 us -> 0.79 us
  local copies, waits for them, and re-layouts: 4.69 us -> 3.07 us
    pallas_call x1, Pallas kernels: 81.5 us -> 88.2 us  [body(): pl.pallas_call(functools.partial(ladder_kernel, n_pair, n_aux, group, win...]
    dot_general x2 -> x0, matrix products: 2.27 us -> none  [the longest x1 1.14 us: body(): jnp.dot(match_first.astype(jnp.bfloat16), singles, preferred_element_type...]
    slice x3 -> x1, local copies, waits for them, and re-layouts: 2.51 us -> 0.8 us  [body(): pair_energy = energies[:, 0, 0]]
    unnamed x5 -> x2, local copies, waits for them, and re-layouts: 1.29 us -> 0.01 us
    convert_element_type x1 -> x0, other arithmetic: 1.25 us -> none  [body(): tau_own = (doubles.astype(jnp.float32) + own_first[:, :, None] * row_seco...]
where the time goes in v2:
time: 92.4 us; the launch traced here: 92.1 us
  Pallas kernels  88.2 us (95%)
  local copies, waits for them, and re-layouts  3.07 us (3%)
    pallas_call x1, Pallas kernels, body(): pl.pallas_call(functools.partial(ladder_kernel, n_pair, n_aux, group, win...  88.2 us

profile of v2, /device:TPU:0, one launch (start us, length us, event | category | flops | bytes accessed | tf_op | source)
XLA Modules:
  0.0 92.1 jit_solution(17069621818259916117)
XLA Ops:
  0.0 0.7 dynamic_slice.11
  0.7 0.0 copy-start
  0.7 88.2 %shard_map.73 = (f32[2,8,256]{2,1,0:T(8,128)}, bf16[2,16,128]{2,1,0:T(8,128)(2,1)}, f32[2,8,128]{2,1,0:T(8,128)}) custom-call(s32[2,2]{1,0:T(2,128)} %pair_ref.1, f32[256]{0:T(256)} %energy_ref.1, bf16[2,256,512]{2,1,0:T(8,128)(2,1)} %doubles_ref.1, bf16[256,512]{1,0:T(8,128)(2,1)} %singles_ref.1, bf16[1024,512]{1,0:T(8,128)(2,1)} %bitcast.3, ...), custom_call_target="tpu_custom_call" | custom-call | flops 25769803776 | bytes 33554432 | tf_op jit(solution)/shard_map/pallas_call | solution.py:429
  89.0 0.7 slice.6
  89.6 0.8 slice_reduce_fusion
  90.4 0.1 broadcast_subtract_fusion
  90.5 0.9 reshape.46
  91.4 0.0 copy-done
  91.4 0.7 divide_add_fusion
  (1 shorter events, 0.0 us)
Async XLA Ops:
  0.7 90.7 %copy-start = (f32[8]{0:T(128)S(1)}, f32[8]{0:T(128)}, u32[]{:S(2)}) copy-start(f32[8]{0:T(128)} %param.12) | copy-start | bytes 100

commit v3 on v2

--- a/solution.py
+++ b/solution.py
@@ -23,7 +23,7 @@
     pair_ref, energy_ref, doubles_ref, singles_ref, vir_hbm, occ_ref,
     out_ref, tile_out_ref, energy_out_ref,
     tau, dressed, slabs, total, fold, parts, tiles, own_ref, vir_ref, outer, lhs_ref,
-    own_sem, vir_sem, slab_sem, z2_send, z2_recv, y2_send, y2_recv, z_send, z_recv, y_send, y_recv,
+    own_sem, vir_sem, slab_sem, z_send, z_recv, y_send, y_recv,
     x_send, x_recv, c_send, c_recv, r_send, r_recv, t_send, t_recv,
 ):
     lines = n_pair // group
@@ -36,7 +36,6 @@
     occ_count = singles_ref.shape[0]
     depth = lhs_ref.shape[1]
     tile_rows, tile_cols = tiles.shape[2:]
-    extra = rows_c // 4 if n_aux > 1 and rows_c % 64 == 0 else 0
     steps = occ_ref.shape[0] // slab_rows
     step_rows = rows // steps
     block = total.shape[1]
@@ -93,49 +92,7 @@
         tau[z, k, own_rows] = (own_ref[k].astype(jnp.float32) + outer[own_rows, :]).astype(jnp.bfloat16)
 
     def piece(zz, k, aa):
-        count = rows_c - extra if k == per_dev - 1 else rows_c
-        return tau.at[zz, k, pl.ds(pl.multiple_of(aa * rows_c, rows_c), count)]
-
-    def last_rows(zz, aa):
-        start = pl.multiple_of(aa * rows_c + rows_c - extra, 16)
-        return tau.at[zz, per_dev - 1, pl.ds(start, extra)]
-
-    def z2_copy(zz, aa, way):
-        ref = last_rows(zz, aa)
-        return pltpu.make_async_remote_copy(
-            src_ref=ref, dst_ref=ref, send_sem=z2_send.at[(way + 1) // 2, zz, aa],
-            recv_sem=z2_recv.at[zz, aa], device_id=at(z + way, g, aux), device_id_type=MESH,
-        )
-
-    def y2_copy(aa, other):
-        ref = last_rows(z, aa)
-        return pltpu.make_async_remote_copy(
-            src_ref=ref, dst_ref=ref, send_sem=y2_send.at[other],
-            recv_sem=y2_recv.at[aa], device_id=at(z, g, other), device_id_type=MESH,
-        )
-
-    def onward2(zz, aa, ways):
-        for way in ways:
-            @pl.when((z + way >= 0) & (z + way < lines))
-            def _():
-                z2_copy(zz, aa, way).start()
-
-    def spread2():
-        for da in range(1, n_aux):
-            source = (aux + da) % n_aux
-            y2_copy(source, source).wait_recv()
-            onward2(z, source, (-1, 1))
-
-    def relay2(dist):
-        for way in (-1, 1):
-            source = z - way * dist
-
-            @pl.when((source >= 0) & (source < lines))
-            def _():
-                for da in range(n_aux):
-                    aa = (aux + da) % n_aux
-                    z2_copy(source, aa, way).wait_recv()
-                    onward2(source, aa, (way,))
+        return tau.at[zz, k, pl.ds(pl.multiple_of(aa * rows_c, rows_c), rows_c)]
 
     def z_copy(zz, k, way):
         ref = piece(zz, k, aux)
@@ -168,9 +125,6 @@
                 z_copy(source, k, way).wait_recv()
                 onward(source, k, (way,))
 
-        if extra and k == per_dev - 1:
-            relay2(dist)
-
     def x_copy(owner_col, part, to_col):
         ref = dressed.at[owner_col * 2 + core, pl.ds(part * send_rows, send_rows)]
         return pltpu.make_async_remote_copy(
@@ -199,13 +153,8 @@
             x_copy(owner, part, owner).wait_recv()
             c_copy(owner, core, part).start()
 
-    if extra:
-        for da in range(1, n_aux):
-            y2_copy(aux, (aux + da) % n_aux).start()
     for k in range(per_dev):
         onward(z, k, (-1, 1))
-    if extra:
-        onward2(z, aux, (-1, 1))
     tiles[aux] = own_ref[:, :tile_rows, :tile_cols]
     for da in range(1, n_aux):
         tile_copy(aux, (aux + da) % n_aux).start()
@@ -237,11 +186,9 @@
         return carry
 
     events = {}
-    if extra:
-        events.setdefault(min(steps, max(1, steps // 5)), []).append(spread2)
     if lines > 1:
         for k in range(per_dev):
-            when = min(steps, max(1, (steps * (7 + 5 * k)) // 16))
+            when = min(steps, max(1, (steps * (9 + 7 * k)) // 16))
             events.setdefault(when, []).append(functools.partial(relay, 1, k))
     passed = 0
     for part in range(sends):
@@ -254,7 +201,7 @@
 
         events.setdefault(made_at, []).append(send_own)
         if part * 2 < sends:
-            later = (part + 1) * steps // sends + (6 * steps) // 16
+            later = (part + 1) * steps // sends + steps // 2
             if later < steps:
                 events.setdefault(later, []).append(functools.partial(pass_block, part))
                 passed = part + 1
@@ -303,31 +250,41 @@
             y_copy(zz, k, source, source).wait_recv()
 
     for k in range(per_dev):
-        if lines > 2:
-            relay(2, k)
         arrived(z, k)
         units(z, k, 0, 1)
         if k == 0:
             for part in range(sends):
                 c_copy(col, 1 - core, part).wait_recv()
         units(z, k, 1, 2)
-        for part in range(passed, min(sends, passed + 1)):
-            pass_block(part)
-            passed = part + 1
+        if k == 0 and passed < sends:
+            pass_block(passed)
+            passed += 1
+    for k in range(per_dev):
+        if lines > 2:
+            relay(2, k)
+        if passed < sends:
+            pass_block(passed)
+            passed += 1
+        if lines > 1:
+            arrived(nth_line(1), k)
+            units(nth_line(1), k, 0, 2)
     for part in range(passed, sends):
         pass_block(part)
     for owner in other_cols():
         for part in range(sends):
             c_copy(owner, 1 - core, part).wait_recv()
     for k in range(per_dev):
+        units(z, k, 2, group)
+    for k in range(per_dev):
         if lines > 3:
             relay(3, k)
-        units(z, k, 2, group)
-    for t in range(1, lines):
+        if lines > 1:
+            units(nth_line(1), k, 2, group)
+    for t in range(2, lines):
         zz = nth_line(t)
         for k in range(per_dev):
-            if t + 3 < lines:
-                relay(t + 3, k)
+            if t + 2 < lines:
+                relay(t + 2, k)
             arrived(zz, k)
             units(zz, k, 0, group)
 
@@ -377,19 +334,6 @@
             x_copy(col, part, to_col).wait_send()
         for dc in range(cols):
             c_copy((col + dc) % cols, core, part).wait_send()
-    if extra:
-        for da in range(1, n_aux):
-            y2_copy(aux, (aux + da) % n_aux).wait_send()
-        for zz in range(lines):
-            @pl.when((zz <= z) & (z + 1 < lines))
-            def _():
-                for aa in range(n_aux):
-                    z2_copy(zz, aa, 1).wait_send()
-
-            @pl.when((zz >= z) & (z >= 1))
-            def _():
-                for aa in range(n_aux):
-                    z2_copy(zz, aa, -1).wait_send()
     for k in range(per_dev):
         for zz in range(lines):
             for da in range(1, n_aux):
@@ -431,7 +375,7 @@
         out_shape=(
             jax.ShapeDtypeStruct((per_dev, win, block), jnp.float32),
             jax.ShapeDtypeStruct(tile_shape, doubles.dtype),
-            jax.ShapeDtypeStruct((per_dev, 8, 128), jnp.float32),
+            jax.ShapeDtypeStruct((per_dev, win // n_aux, win), jnp.float32),
         ),
         in_specs=[smem, smem, anywhere, vmem, anywhere, anywhere],
         out_specs=(vmem, vmem, vmem),
@@ -448,7 +392,6 @@
             pltpu.VMEM((width, width), jnp.float32),
             pltpu.VMEM((2 * win, 2 * occ_count), jnp.bfloat16),
             dma, dma, dma((slots,)),
-            dma((2, lines, n_aux)), dma((lines, n_aux)), dma((n_aux,)), dma((n_aux,)),
             dma((2, lines, per_dev)), dma((lines, per_dev)),
             dma((lines, per_dev, n_aux)), dma((lines, per_dev, n_aux)),
             dma((cols, sends)), dma((cols, sends)),
@@ -474,8 +417,7 @@
     share = lax.dynamic_slice_in_dim(residual, row_start, share_rows, 1)
     own_doubles = lax.dynamic_slice_in_dim(tiles[:, :win, :win], row_start, share_rows, 1)
     own_vir = lax.dynamic_slice_in_dim(vir_energy, row_start, share_rows, 0)
-    pair_energy = energies[:, 0, 0]
-    denominator = pair_energy[:, None, None] - own_vir[None, :, None] - vir_energy[None, None, :]
+    denominator = energies - own_vir[None, :, None] - vir_energy[None, None, :]
     return own_doubles.astype(jnp.float32) + share / denominator
 
 

time: 92.4 us -> 87.8 us (0.950)
  Pallas kernels: 88.2 us -> 83.8 us
    pallas_call x1, Pallas kernels: 88.2 us -> 83.8 us  [body(): pl.pallas_call(functools.partial(ladder_kernel, n_pair, n_aux, group, win...]
where the time goes in v3:
time: 87.8 us; the launch traced here: 87.5 us
  Pallas kernels  83.8 us (95%)
  local copies, waits for them, and re-layouts  2.28 us (3%)
  other arithmetic  1.39 us (2%)
    pallas_call x1, Pallas kernels, body(): pl.pallas_call(functools.partial(ladder_kernel, n_pair, n_aux, group, win...  83.8 us

profile of v3, /device:TPU:0, one launch (start us, length us, event | category | flops | bytes accessed | tf_op | source)
XLA Modules:
  0.0 87.5 jit_solution(7489588484781780061)
XLA Ops:
  0.0 0.7 dynamic_slice.11
  0.7 0.0 copy-start
  0.7 83.8 %shard_map.73 = (f32[2,8,256]{2,1,0:T(8,128)}, bf16[2,16,128]{2,1,0:T(8,128)(2,1)}, f32[2,4,8]{2,1,0:T(4,128)}) custom-call(s32[2,2]{1,0:T(2,128)} %pair_ref.1, f32[256]{0:T(256)} %energy_ref.1, bf16[2,256,512]{2,1,0:T(8,128)(2,1)} %doubles_ref.1, bf16[256,512]{1,0:T(8,128)(2,1)} %singles_ref.1, bf16[1024,512]{1,0:T(8,128)(2,1)} %bitcast.3, ...), custom_call_target="tpu_custom_call" | custom-call | flops 25769803776 | bytes 33554432 | tf_op jit(solution)/shard_map/pallas_call | solution.py:373
  84.6 0.7 slice.3
  85.2 0.9 reshape.13
  86.2 0.0 copy-done
  86.2 1.4 %divide_add_fusion = f32[2,4,8]{2,1,0:T(4,128)} fusion(f32[2,4,8]{2,1,0:T(4,128)} %get-tuple-element.10, f32[2,8,8]{2,1,0:T(8,128)S(1)} %reduce_sum.9, s32[]{:T(128)S(6)} %select_n.2, f32[8]{0:T(128)S(1)} %copy-done, f32[4]{0:T(128)S(1)} %dynamic_slice.11, bf16[2,8,8]{2,1,0:T(8,128)(2,1)S(1)} %slice.3), kind=kLoop, calls=%fused_computation | loop fusion | flops 320 | bytes 948 | tf_op jit(solution)/shard_map/add | solution.py:421
  (1 shorter events, 0.0 us)
Async XLA Ops:
  0.7 85.4 %copy-start = (f32[8]{0:T(128)S(1)}, f32[8]{0:T(128)}, u32[]{:S(2)}) copy-start(f32[8]{0:T(128)} %param.12) | copy-start | bytes 100
